TPU v7x, 32 devices: a whole 2x2x4 slice. The times are simulated.
32 devices in a mesh: section: 2 (over x), seq: 4 (over y, core), dp: 4 (over z).
Axes of the slice: x: 2, y: 2, z: 4, core: 2. Of those that a mesh axis runs over, the one named last changes fastest.
Arguments:
- boundary: bfloat16 [2, 16, 1024, 1280], P('section', 'dp', 'seq'), may hold values from -6 to 6
- lengths: int32 [16, 4], P('dp'), may hold values from 0 to 1024, as said below
- masked: int32 [16, 1024], P('dp', 'seq'), may hold values 0 or 1
- residues: int32 [16, 1024], P('dp', 'seq'), may hold values from 0 to 29
- readout: bfloat16 [1280, 30], replicated, may hold values from -0.15625 to 0.15625
- first_gain: float32 [2, 1280], P('section'), may hold values from 0.5 to 1.5
- first_shift: float32 [2, 1280], P('section'), may hold values from -2 to 2
- in_weight: bfloat16 [2, 1280, 640], P('section'), may hold values from -0.15625 to 0.15625
- in_bias: float32 [2, 640], P('section'), may hold values from -2 to 2
- second_gain: float32 [2, 640], P('section'), may hold values from 0.5 to 1.5
- second_shift: float32 [2, 640], P('section'), may hold values from -2 to 2
- conv_weight: bfloat16 [2, 5, 640, 640], P('section'), may hold values from -0.109375 to 0.109375
- conv_bias: float32 [2, 640], P('section'), may hold values from -2 to 2
- third_gain: float32 [2, 640], P('section'), may hold values from 0.5 to 1.5
- third_shift: float32 [2, 640], P('section'), may hold values from -2 to 2
- out_weight: bfloat16 [2, 640, 1280], P('section'), may hold values from -0.25 to 0.25
- out_bias: float32 [2, 1280], P('section'), may hold values from -2 to 2
Outputs:
- boundary_out: bfloat16 [2, 16, 1024, 1280], P('section', 'dp', 'seq')
- grad_first_gain: float32 [2, 1280], P('section')
- grad_first_shift: float32 [2, 1280], P('section')
- grad_in_weight: float32 [2, 1280, 640], P('section')
- grad_in_bias: float32 [2, 640], P('section')
- grad_second_gain: float32 [2, 640], P('section')
- grad_second_shift: float32 [2, 640], P('section')
- grad_conv_weight: float32 [2, 5, 640, 640], P('section')
- grad_conv_bias: float32 [2, 640], P('section')
- grad_third_gain: float32 [2, 640], P('section')
- grad_third_shift: float32 [2, 640], P('section')
- grad_out_weight: float32 [2, 640, 1280], P('section')
- grad_out_bias: float32 [2, 1280], P('section')
- type_scores: float32 [30], replicated
- type_counts: int32 [30], replicated
Inputs may be any that keep to these rules, and one draw needn't show every extreme that they name: `lengths`: the items of a row lie one after another from position 0 and the rest of the row is padding; in each aligned block of 4 rows one row is a single item of 1024 positions.
All inputs are finite; a program needn't handle non-finite values. No bound on the sum of `masked` on one device may be relied on, other than what follows from the above.
Results may differ from a plain program's by a relative error of at most 0.012.
Values may be sent and summed in bfloat16 or wider, within the bound.
A program may use at most 256 MiB of HBM per device.

v0:
```python
import functools

import jax
import jax.numpy as jnp
from jax import lax
from jax.experimental import pallas as pl
from jax.experimental.pallas import tpu as pltpu
from jax.sharding import PartitionSpec as P

KERNEL = 5
VOCAB = 30
DILATION_STEP = 128
ITEMS = 4
EPSILON = 1e-05
ROOT_HALF = 0.7071067811865476
HALF_LOG = -0.7213475204444817
ROOT_TAU = 0.3989422804014327

MESH = pl.DeviceIdType.MESH
LANES = 2
LOADS_AHEAD = 4
VMEM_BYTES = 64 << 20


def far_rows(left, own, right, offset):
    edge, positions = left.shape[0], own.shape[0]
    first, last = offset + edge, offset + edge + positions
    pieces, at = [], 0
    for block in (left, own, right):
        lo, hi = max(first, at), min(last, at + block.shape[0])
        if lo < hi:
            pieces.append(block[lo - at : hi - at])
        at += block.shape[0]
    return pieces[0] if len(pieces) == 1 else jnp.concatenate(pieces, axis=0)


def act_forward(values, gain, shift, real):
    scale = 1.0 / values.shape[1]
    centred = values - jnp.sum(values, axis=1, keepdims=True) * scale
    spread = jnp.sum(centred * centred, axis=1, keepdims=True) * scale
    inverse = lax.rsqrt(spread + EPSILON)
    hat = centred * inverse
    moved = hat * gain + shift
    below = (0.5 + 0.5 * lax.erf(moved * ROOT_HALF)) * real
    density = jnp.exp2(moved * moved * HALF_LOG) * (ROOT_TAU * real)
    return moved * below, hat, below + moved * density, inverse


def fold(values):
    rows, columns = values.shape
    return jnp.sum(values.reshape(rows // 8, 8, columns), axis=0)


def act_backward(grad, hat, slope, inverse, gain, gain_sum, shift_sum):
    scale = 1.0 / grad.shape[1]
    hat = hat.astype(jnp.float32)
    moved = grad * slope.astype(jnp.float32)
    turned = moved * hat
    shift_sum[...] += fold(moved)
    gain_sum[...] += fold(turned)
    mean = jnp.sum(moved * gain, axis=1, keepdims=True) * scale
    tilt = jnp.sum(turned * gain, axis=1, keepdims=True) * scale
    return inverse * (moved * gain - mean - hat * tilt)


def dot_nn(a, b):
    return jnp.dot(a, b, preferred_element_type=jnp.float32)


def dot_nt(a, b):
    return lax.dot_general(a, b, (((1,), (1,)), ((), ())), preferred_element_type=jnp.float32)


def dot_tn(a, b):
    return lax.dot_general(a, b, (((0,), (0,)), ((), ())), preferred_element_type=jnp.float32)


def blocks_kernel(
    edge, plan,
    boundary, lengths, masked, residues, readout,
    first_gain, first_shift, in_weight, in_bias, second_gain, second_shift, conv_weight, conv_bias,
    third_gain, third_shift, out_weight, out_bias,
    result, big, small_out,
    buf, w_in, w_conv, w_out, total, hat1, slope1, act1, taps, back_taps,
    hat2, slope2, hat3, slope3, act3, rim_left, rim_right, near, masks,
    sums_wide, sums, hits, tally, core_land, small, small_land,
    load_sem, weight_sem, result_sem, hand_send, hand_recv, rim_send, rim_recv, small_send, small_recv, *ring_refs,
):
    grad1, grad2 = hat2, hat3
    section = lax.axis_index("section")
    seq = lax.axis_index("seq")
    dp = lax.axis_index("dp")
    n_seq = lax.axis_size("seq")
    rows, positions = buf.shape[0] // 2, buf.shape[1]
    hidden = w_in.shape[1]
    leading = section == 0
    trailing = section == 1
    row_len = n_seq * positions
    first_position = seq * positions
    reach = edge // positions
    dilation = jnp.where(leading, 1, DILATION_STEP)

    def load(m):
        return pltpu.make_async_copy(boundary.at[0, m], buf.at[section * rows + m], load_sem.at[m])

    weight_loads = [
        pltpu.make_async_copy(source.at[0], target, weight_sem.at[i])
        for i, (source, target) in enumerate(((in_weight, w_in), (conv_weight, w_conv), (out_weight, w_out)))
    ]
    load(0).start()
    weight_loads[0].start()

    def partner():
        return (1 - section, seq, dp)

    rings, at = [], 0
    for sizes, base, land in plan:
        ring = Ring(sizes, base, land, section, seq, dp, n_seq // 2, lax.axis_size("dp"))
        ring.bind(total, taps, core_land, big, ring_refs[at : at + ring.refs])
        at += ring.refs
        rings.append(ring)
    barrier = pltpu.get_barrier_semaphore()
    greet = [partner()] + rings[0].neighbours()
    for peer in greet:
        pl.semaphore_signal(barrier, inc=1, device_id=peer, device_id_type=MESH)
    greeted = len(greet)
    for j in range(1, reach + 1):
        for side in (-j, j):
            on = (seq + side >= 0) & (seq + side < n_seq)
            greeted = greeted + on.astype(jnp.int32)

            @pl.when(on)
            def _():
                pl.semaphore_signal(barrier, inc=1, device_id=(section, seq + side, dp), device_id_type=MESH)

    @pl.when(seq < reach)
    def _():
        rim_left[...] = jnp.zeros_like(rim_left)

    @pl.when(seq >= n_seq - reach)
    def _():
        rim_right[...] = jnp.zeros_like(rim_right)

    last = rows - 1
    half, quarter = positions // 2, positions // 4
    parts = ((0, half), (half, half))
    thirds = ((quarter, half), (0, quarter), (half + quarter, quarter))
    whole = ((0, positions),)

    def make_mask(m):
        lane = lax.broadcasted_iota(jnp.int32, (positions, 128), 1)
        place = lax.broadcasted_iota(jnp.int32, (positions, 128), 0) + first_position
        other = place + (lane - KERNEL // 2) * dilation
        end = 0
        here = jnp.zeros((positions, 128), jnp.int32)
        there = jnp.zeros((positions, 128), jnp.int32)
        for j in range(ITEMS):
            end = end + lengths[m, j]
            here = here + (place >= end).astype(jnp.int32)
            there = there + (other >= end).astype(jnp.int32)
        counts = (here == there) & (here < ITEMS) & (other >= 0) & (other < row_len)
        masks[m] = counts.astype(jnp.float32)

    def hand(source, m, part):
        first, count = (thirds if source is buf else parts)[part]
        block = pl.ds(first, count)
        target = buf.at[m, block] if source is buf else buf.at[rows + m, block]
        return pltpu.make_async_remote_copy(
            src_ref=source.at[m, block], dst_ref=target,
            send_sem=hand_send.at[m, part], recv_sem=hand_recv.at[m, part],
            device_id=partner(), device_id_type=MESH)

    def tap_rows(m, k, first=0, count=None):
        start = (m * KERNEL + k) * positions + first
        return pl.ds(pl.multiple_of(start, 16), positions if count is None else count)

    def near_copies(backward, m):
        slot = 2 * backward + m % 2
        turn = backward * rows + m

        def edge_rows(first):
            return grad2.at[m, pl.ds(first, 16)] if backward else taps.at[tap_rows(m, KERNEL // 2, first, 16)]

        def copy(source, target, index, to):
            return pltpu.make_async_remote_copy(
                src_ref=source, dst_ref=target, send_sem=rim_send.at[turn, index], recv_sem=rim_recv.at[turn, index],
                device_id=(section, to, dp), device_id_type=MESH)

        return [
            (seq + 1 < n_seq, seq >= 1,
             copy(edge_rows(positions - 16), rim_left.at[slot, pl.ds(edge - 16, 16)], 0, seq + 1)),
            (seq >= 1, seq + 1 < n_seq,
             copy(edge_rows(0), rim_right.at[slot, pl.ds(0, 16)], 1, seq - 1)),
        ]

    def far_copies(backward, m, part, pieces):
        first, count = pieces[part]
        slot = 2 * backward + m % 2
        turn = backward * rows + m
        own = grad2.at[m, pl.ds(first, count)] if backward else taps.at[tap_rows(m, KERNEL // 2, first, count)]

        def copy(target, index, to):
            return pltpu.make_async_remote_copy(
                src_ref=own, dst_ref=target,
                send_sem=rim_send.at[turn, 3 * index + part], recv_sem=rim_recv.at[turn, 3 * index + part],
                device_id=(section, to, dp), device_id_type=MESH)

        copies = []
        for j in range(1, reach + 1):
            copies.append((
                seq + j < n_seq, seq >= j,
                copy(rim_left.at[slot, pl.ds(edge - j * positions + first, count)], 2 * j - 2, seq + j)))
            copies.append((
                seq >= j, seq + j < n_seq,
                copy(rim_right.at[slot, pl.ds((j - 1) * positions + first, count)], 2 * j - 1, seq - j)))
        return copies

    def begin(copies):
        for sends, _, copy in copies:
            pl.when(sends)(copy.start)

    def end(copies):
        for sends, receives, copy in copies:
            pl.when(receives)(copy.wait_recv)
            pl.when(sends)(copy.wait_send)

    def gather_near(backward, m, own, store, rims):
        slot = 2 * backward + m % 2
        if not rims:
            near[16 : 16 + positions] = own.astype(jnp.float32)
            pieces = thirds[:1]
        else:
            near[0:16] = rim_left[slot, edge - 16 : edge].astype(jnp.float32)
            near[16 + positions : 32 + positions] = rim_right[slot, 0:16].astype(jnp.float32)
            pieces = thirds[1:]
        for first, count in pieces:
            mask = masks[m, first : first + count]
            for k in range(KERNEL):
                if k != KERNEL // 2:
                    at = 16 + first + k - KERNEL // 2
                    store(k, first, jnp.where(mask[:, k : k + 1] > 0, near[at : at + count], 0.0))

    def gather_far(backward, m, own, store):
        slot = 2 * backward + m % 2
        mask = masks[m]
        for k in range(KERNEL):
            if k != KERNEL // 2:
                piece = far_rows(rim_left[slot], own, rim_right[slot], (k - KERNEL // 2) * DILATION_STEP)
                store(k, 0, jnp.where(mask[:, k : k + 1] > 0, piece.astype(jnp.float32), 0.0))

    def store_tap(m):
        def store(k, first, value):
            taps[tap_rows(m, k, first, value.shape[0])] = value.astype(jnp.bfloat16)

        return store

    def store_back(k, first, value):
        back_taps[k - (k > KERNEL // 2), first : first + value.shape[0]] = value.astype(jnp.bfloat16)

    def front(m, piece):
        block = slice(piece[0], piece[0] + piece[1])
        real = masks[m, block, KERNEL // 2 : KERNEL // 2 + 1]
        act, hat, slope, inverse = act_forward(
            buf[m, block].astype(jnp.float32), first_gain[...], first_shift[...], real)
        act1[m, block] = act.astype(jnp.bfloat16)
        hat1[m, block] = hat.astype(jnp.bfloat16)
        slope1[m, block] = slope.astype(jnp.bfloat16)
        masks[m, block, 8:9] = inverse
        pre = dot_nn(act1[m, block], w_in[...]) + in_bias[...]
        act, hat, slope, inverse = act_forward(pre, second_gain[...], second_shift[...], real)
        taps[tap_rows(m, KERNEL // 2, *piece)] = act.astype(jnp.bfloat16)
        hat2[m, block] = hat.astype(jnp.bfloat16)
        slope2[m, block] = slope.astype(jnp.bfloat16)
        masks[m, block, 9:10] = inverse

    def middle_tap(m, piece):
        return conv_bias[...] + dot_nn(taps[tap_rows(m, KERNEL // 2, *piece)], w_conv[KERNEL // 2])

    def rear(m, piece, pre):
        block = slice(piece[0], piece[0] + piece[1])
        for k in range(KERNEL):
            if k != KERNEL // 2:
                pre = pre + dot_nn(taps[tap_rows(m, k, *piece)], w_conv[k])
        real = masks[m, block, KERNEL // 2 : KERNEL // 2 + 1]
        act, hat, slope, inverse = act_forward(pre, third_gain[...], third_shift[...], real)
        act3[m, block] = act.astype(jnp.bfloat16)
        hat3[m, block] = hat.astype(jnp.bfloat16)
        slope3[m, block] = slope.astype(jnp.bfloat16)
        masks[m, block, 10:11] = inverse
        out = buf[m, block].astype(jnp.float32) + (dot_nn(act3[m, block], w_out[...]) + out_bias[...])
        buf[m, block] = out.astype(jnp.bfloat16)

    def count_types(m):
        logits = dot_nt(readout[...], buf[m])
        kind = lax.broadcasted_iota(jnp.int32, logits.shape, 0)
        odds = jnp.exp(logits - jnp.max(logits, axis=0, keepdims=True))
        odds = odds / jnp.sum(odds, axis=0, keepdims=True)
        stop = lengths[m, 0]
        for j in range(1, ITEMS):
            stop = stop + lengths[m, j]
        spot = lax.broadcasted_iota(jnp.int32, (1, positions), 1) + first_position
        chosen = jnp.where(spot < stop, masked[pl.ds(m, 1)].astype(jnp.float32), 0.0)
        chosen = jnp.where(kind == residues[pl.ds(m, 1)], chosen, 0.0)
        hits[...] += chosen * odds
        tally[...] += chosen

    def back_front(m, piece):
        block = slice(piece[0], piece[0] + piece[1])
        sums_wide[2] += fold(buf[rows + m, block].astype(jnp.float32))
        grad = dot_nt(buf[rows + m, block], w_out[...])
        low = act_backward(
            grad, hat3[m, block], slope3[m, block], masks[m, block, 10:11], third_gain[...], sums.at[4], sums.at[5]
        ).astype(jnp.bfloat16)
        grad2[m, block] = low
        sums[3] += fold(low.astype(jnp.float32))

    def back_middle_tap(m):
        return dot_nt(grad2[m], w_conv[KERNEL // 2])

    def back_rear(m, grad, between=None):
        for k in range(KERNEL):
            if k != KERNEL // 2:
                grad = grad + dot_nt(back_taps[k - (k > KERNEL // 2)], w_conv[KERNEL - 1 - k])
        if between is not None:
            between()
        low = act_backward(
            grad, hat2[m], slope2[m], masks[m, :, 9:10], second_gain[...], sums.at[1], sums.at[2]
        ).astype(jnp.bfloat16)
        grad1[m] = low
        sums[0] += fold(low.astype(jnp.float32))

    def back_last(m, piece):
        block = slice(piece[0], piece[0] + piece[1])
        grad = dot_nt(grad1[m, block], w_in[...])
        grad = act_backward(
            grad, hat1[m, block], slope1[m, block], masks[m, block, 8:9], first_gain[...],
            sums_wide.at[0], sums_wide.at[1])
        hat1[m, block] = (buf[rows + m, block].astype(jnp.float32) + grad).astype(jnp.bfloat16)

    def give(source, m):
        return pltpu.make_async_copy(source.at[m], result.at[0, m], result_sem.at[m])

    wide = buf.shape[2] // hidden

    def add_block(start, value):
        total[pl.ds(start, hidden)] += value

    def weights_out(m):
        for j in range(wide):
            add_block((KERNEL + j) * hidden, dot_tn(act3[m], buf[rows + m, :, j * hidden : (j + 1) * hidden]))

    def weights_conv(m):
        for k in range(KERNEL):
            add_block(k * hidden, dot_tn(taps[tap_rows(m, k)], grad2[m]))

    def weights_in(m):
        for j in range(wide):
            add_block(rings[1].base + j * hidden, dot_tn(act1[m, :, j * hidden : (j + 1) * hidden], grad1[m]))

    def first_lane():
        rings[0].exchange(2)
        rings[0].towards(0, 0, True)

    def step(i, carry):
        fronts = i < rows
        m_start = jnp.where(leading, i - rows, i)
        m_end = m_start - 1
        m_sum = i - rows
        final = i == 2 * rows

        def on(m):
            return (m >= 0) & (m < rows)

        @pl.when(fronts)
        def _():
            make_mask(i)

        @pl.when(i == 0)
        def _():
            weight_loads[0].wait()
            for copy in weight_loads[1:]:
                copy.start()

        @pl.when(leading & fronts)
        def _():
            load(i).wait()

        @pl.when(i == 0)
        def _():
            for m in range(1, rows):
                load(m).start()

        @pl.when(trailing & (i < last))
        def _():
            for part in range(3):
                hand(buf, i, part).wait_recv()

        @pl.when(fronts & (leading | (i < last)))
        def _():
            front(i, whole[0])

        @pl.when(i == 0)
        def _():
            pl.semaphore_wait(barrier, greeted)

        @pl.when(leading & fronts)
        def _():
            begin(near_copies(0, i))

        @pl.when(trailing & (i < last))
        def _():
            begin(far_copies(0, i, 0, whole))

        @pl.when(trailing & (i == last))
        def _():
            for part in range(3):
                hand(buf, last, part).wait_recv()
                front(last, thirds[part])
                begin(far_copies(0, last, part, thirds))

        @pl.when(i == 0)
        def _():
            weight_loads[1].wait()
            weight_loads[2].wait()

        @pl.when(on(m_end))
        def _():
            grad = back_middle_tap(m_end)

            @pl.when(leading)
            def _():
                gather_near(1, m_end, grad2[m_end], store_back, False)
                end(near_copies(1, m_end))
                gather_near(1, m_end, grad2[m_end], store_back, True)

            @pl.when(trailing)
            def _():
                for part in range(2):
                    end(far_copies(1, m_end, part, parts))
                gather_far(1, m_end, grad2[m_end], store_back)

            back_rear(m_end, grad, lambda: pl.when(final)(first_lane))
            for part in range(2):
                back_last(m_end, parts[part])
                pl.when(trailing)(hand(hat1, m_end, part).start)
            pl.when(leading)(give(hat1, m_end).start)

        @pl.when(trailing & final)
        def _():
            first_lane()

        @pl.when(on(m_sum - 1))
        def _():
            weights_in(m_sum - 1)

        @pl.when(final)
        def _():
            for lane in range(1, rings[0].lanes):
                rings[0].towards(0, lane, True)
            rings[1].exchange(0)
            rings[1].exchange(1)

        @pl.when(leading & fronts)
        def _():
            gather_near(0, i, taps[tap_rows(i, KERNEL // 2)], store_tap(i), False)
            rear(i, thirds[0], middle_tap(i, thirds[0]))
            hand(buf, i, 0).start()
            end(near_copies(0, i))
            gather_near(0, i, taps[tap_rows(i, KERNEL // 2)], store_tap(i), True)
            for part in (1, 2):
                rear(i, thirds[part], middle_tap(i, thirds[part]))
                hand(buf, i, part).start()

        @pl.when((leading & (i == 2)) | (trailing & (i == 0)))
        def _():
            total[...] = jnp.zeros_like(total)
            sums_wide[...] = jnp.zeros_like(sums_wide)
            sums[...] = jnp.zeros_like(sums)
            hits[...] = jnp.zeros_like(hits)
            tally[...] = jnp.zeros_like(tally)

        @pl.when(trailing & fronts)
        def _():
            pre = middle_tap(i, whole[0])

            @pl.when(i < last)
            def _():
                end(far_copies(0, i, 0, whole))

            @pl.when(i == last)
            def _():
                for part in range(3):
                    end(far_copies(0, last, part, thirds))

            gather_far(0, i, taps[tap_rows(i, KERNEL // 2)], store_tap(i))
            rear(i, whole[0], pre)
            give(buf, i).start()

        @pl.when(on(m_start))
        def _():
            pl.when(trailing)(load(m_start).wait)
            for part in range(2):
                pl.when(leading)(hand(hat1, m_start, part).wait_recv)
                back_front(m_start, parts[part])

                @pl.when(trailing)
                def _():
                    begin(far_copies(1, m_start, part, parts))

            @pl.when(leading)
            def _():
                begin(near_copies(1, m_start))

        @pl.when(trailing & fronts)
        def _():
            count_types(i)

        @pl.when(on(m_sum))
        def _():
            weights_out(m_sum)
            weights_conv(m_sum)

        @pl.when(i == 2 * rows - 1)
        def _():
            rings[0].exchange(0)
            rings[0].exchange(1)

        return carry

    lax.fori_loop(0, 2 * rows + 1, step, 0)

    for i in range(3):
        small[i : i + 1, :] = jnp.sum(sums_wide[i], axis=0, keepdims=True)
    for i in range(6):
        small[3 + i // 2 : 4 + i // 2, (i % 2) * hidden : (i % 2 + 1) * hidden] = jnp.sum(sums[i], axis=0, keepdims=True)
    small[6:8, :] = jnp.zeros((2, small.shape[1]), jnp.float32)
    ones = jnp.ones((8, positions), jnp.float32)
    for i, counted in ((6, hits), (7, tally)):
        row = lax.dot_general(
            ones, counted[...], (((1,), (1,)), ((), ())), precision=lax.Precision.HIGHEST,
            preferred_element_type=jnp.float32)
        small[i : i + 1, 0 : counted.shape[0]] = row[0:1]
    run_rings(rings, SmallSum(rings[0], small, small_land, small_out, small_send, small_recv, partner()))
    for m in range(rows):
        @pl.when(leading)
        def _():
            for part in range(3):
                hand(buf, m, part).wait_send()
            give(hat1, m).wait()

        @pl.when(trailing)
        def _():
            for part in range(2):
                hand(hat1, m, part).wait_send()
            give(buf, m).wait()


def ring_plan(width, hidden, nodes):
    plan, base, land = [], 0, 0
    for rows, subs in (((KERNEL + width // hidden) * hidden, LANES), (width, 1)):
        sizes = ring_sizes(rows // 2, nodes, subs)
        plan.append((sizes, base, land))
        land += nodes * sum(map(sum, sizes))
        base = 2 * land
    return plan, land


def run_blocks(args, ny, nz, cid=0):
    nodes = ny * nz
    doublings = 1 + (ny - 1).bit_length() + (nz - 1).bit_length()
    boundary, in_weight, conv_weight = args[0], args[7], args[11]
    _, rows, positions, width = boundary.shape
    hidden = in_weight.shape[2]
    edge = KERNEL // 2 * DILATION_STEP
    assert edge % positions == 0 and positions % 32 == 0 and width % hidden == 0
    reach = edge // positions
    low, full = jnp.bfloat16, jnp.float32
    wide_rows = pltpu.VMEM((rows, positions, width), low)
    thin_rows = pltpu.VMEM((rows, positions, hidden), low)
    plan, half = ring_plan(width, hidden, nodes)
    where = [pltpu.HBM, pltpu.SMEM] + [pltpu.VMEM] * 15
    for i in (7, 11, 15):
        where[i] = pltpu.HBM
    return pl.pallas_call(
        functools.partial(blocks_kernel, edge, plan),
        out_shape=(
            jax.ShapeDtypeStruct(boundary.shape, low),
            jax.ShapeDtypeStruct((2 * half, hidden), low),
            jax.ShapeDtypeStruct((16, width), full),
        ),
        in_specs=[pl.BlockSpec(memory_space=space) for space in where],
        out_specs=[pl.BlockSpec(memory_space=space) for space in (pltpu.HBM, pltpu.HBM, pltpu.VMEM)],
        scratch_shapes=[
            pltpu.VMEM((2 * rows, positions, width), low),
            pltpu.VMEM((width, hidden), low),
            pltpu.VMEM((KERNEL, hidden, hidden), low),
            pltpu.VMEM((hidden, width), low),
            pltpu.VMEM((2 * half, hidden), full),
            wide_rows, wide_rows, wide_rows,
            pltpu.VMEM((max(rows * KERNEL * positions, half), hidden), low),
            pltpu.VMEM((KERNEL - 1, positions, hidden), low),
            thin_rows, thin_rows, thin_rows, thin_rows, thin_rows,
            pltpu.VMEM((4, edge, hidden), low),
            pltpu.VMEM((4, edge, hidden), low),
            pltpu.VMEM((positions + 32, hidden), full),
            pltpu.VMEM((rows, positions, 128), full),
            pltpu.VMEM((3, 8, width), full),
            pltpu.VMEM((6, 8, hidden), full),
            pltpu.VMEM((VOCAB, positions), full),
            pltpu.VMEM((VOCAB, positions), full),
            pltpu.VMEM((half, hidden), low),
            pltpu.VMEM((8, width), full),
            pltpu.VMEM((2 * doublings, 8, width), full),
            pltpu.SemaphoreType.DMA((rows,)),
            pltpu.SemaphoreType.DMA((3,)),
            pltpu.SemaphoreType.DMA((rows,)),
            pltpu.SemaphoreType.DMA((rows, 3)),
            pltpu.SemaphoreType.DMA((rows, 3)),
            pltpu.SemaphoreType.DMA((2 * rows, 6 * reach)),
            pltpu.SemaphoreType.DMA((2 * rows, 6 * reach)),
            pltpu.SemaphoreType.DMA((doublings + 1,)),
            pltpu.SemaphoreType.DMA((doublings + 1,)),
        ]
        + [scratch for sizes, _, _ in plan for scratch in ring_scratch(sizes, nodes, hidden)],
        compiler_params=pltpu.CompilerParams(
            collective_id=cid, has_side_effects=True, vmem_limit_bytes=VMEM_BYTES),
    )(*args)


def ring_sizes(rows, nodes, subs):
    units = -(-rows // (nodes * 16))
    long = -(-units // 2)
    return [[16 * ((way + i) // subs) for i in range(subs)] for way in (long, units - long)]


def ring_flows(sizes):
    return [(way, i) for i in range(len(sizes[0])) for way in range(2) if sizes[way][i]]


def ring_scratch(sizes, nodes, columns):
    flows = ring_flows(sizes)
    n = len(flows)
    counts = [(n, nodes)] * 2 + [(n, 2 * nodes - 2)] * 2 + [(n, nodes)] * 2 + [(n,)]
    return [pltpu.SemaphoreType.DMA(count) for count in counts] + [
        pltpu.VMEM((nodes - 1, sizes[way][i], columns), jnp.bfloat16) for way, i in flows]


class Ring:
    def __init__(self, sizes, base, land, section, seq, dp, ny, nz):
        self.sizes, self.base, self.land, self.nodes = sizes, base, land, ny * nz
        self.flows = ring_flows(sizes)
        self.refs = 7 + len(self.flows)
        self.lanes = len(sizes[0])
        self.section, self.nz = section, nz
        self.core, ypos = seq % 2, seq // 2
        self.spot = ypos * nz + dp + (ypos % 2) * (nz - 1 - 2 * dp)
        self.other_core = (section, seq + 1 - 2 * self.core, dp)
        self.turn = [1 - 2 * self.core, 2 * self.core - 1]
        self.next = [self.at_spot(self.wrap(self.spot + self.nodes + turn)) for turn in self.turn]
        self.half = sum(map(sum, sizes)) * self.nodes
        self.first, at = {}, 0
        for way, i in self.flows:
            self.first[way, i] = at
            at += sizes[way][i] * self.nodes
        self.peers = [self.other_core]
        reach = 1
        while reach < ny:
            self.peers.append((section, seq + 2 * reach - 4 * reach * ((ypos // reach) % 2), dp))
            reach *= 2
        reach = 1
        while reach < nz:
            self.peers.append((section, seq, dp + reach - 2 * reach * ((dp // reach) % 2)))
            reach *= 2

    def wrap(self, place):
        if self.nodes & (self.nodes - 1) == 0:
            return place & (self.nodes - 1)
        return lax.rem(place, self.nodes)

    def at_spot(self, place):
        y = place // self.nz
        z = place % self.nz
        return (self.section, y * 2 + self.core, z + (y % 2) * (self.nz - 1 - 2 * z))

    def neighbours(self):
        around = self.next
        return self.peers + around

    def bind(self, total, stage, core_land, big, refs):
        self.total, self.stage, self.core_land, self.big = total, stage, core_land, big
        self.core_sems, self.ring_sems, self.over_sems = refs[0:2], refs[2:4], refs[4:6]
        self.keep_sem, self.lands = refs[6], refs[7:]

    def count(self, f):
        way, i = self.flows[f]
        return self.sizes[way][i]

    def rows(self, f, side, shard):
        start = self.base + side * self.half + self.first[self.flows[f]] + shard * self.count(f)
        return pl.ds(pl.multiple_of(start, 16), self.count(f))

    def land_rows(self, f, shard):
        start = self.land + self.first[self.flows[f]] + shard * self.count(f)
        return pl.ds(pl.multiple_of(start, 16), self.count(f))

    def shard(self, f, step):
        return self.wrap(self.spot + 2 * self.nodes - self.turn[self.flows[f][0]] * step)

    def ahead(self, f):
        return self.next[self.flows[f][0]]

    def remote(self, source, target, sems, index, peer):
        return pltpu.make_async_remote_copy(
            src_ref=source, dst_ref=target, send_sem=sems[0].at[index], recv_sem=sems[1].at[index],
            device_id=peer, device_id_type=MESH)

    def core_copy(self, f, shard):
        rows = self.land_rows(f, shard)
        return self.remote(self.stage.at[rows], self.core_land.at[rows], self.core_sems, (f, shard), self.other_core)

    def ring_copy(self, f, step, shard):
        return self.remote(
            self.core_land.at[self.land_rows(f, shard)], self.lands[f].at[step], self.ring_sems, (f, step), self.ahead(f))

    def back_copy(self, f, step, shard):
        block = self.big.at[self.rows(f, self.core, shard)]
        return self.remote(
            self.core_land.at[self.land_rows(f, shard)] if step is None else block, block,
            self.ring_sems, (f, self.nodes - 1 + (0 if step is None else step)), self.ahead(f))

    def over_copy(self, f, shard, own=False):
        block = self.big.at[self.rows(f, self.core, shard)]
        return self.remote(
            self.core_land.at[self.land_rows(f, shard)] if own else block, block,
            self.over_sems, (f, shard), self.other_core)

    def keep_copy(self, f, shard):
        return pltpu.make_async_copy(
            self.core_land.at[self.land_rows(f, shard)], self.big.at[self.rows(f, self.core, shard)], self.keep_sem.at[f])

    def add(self, f, shard, step):
        rows = self.land_rows(f, shard)
        value = self.total[self.rows(f, self.core, shard)] + self.core_land[rows].astype(jnp.float32)
        if step is not None:
            value = value + self.lands[f][step].astype(jnp.float32)
        self.core_land[rows] = value.astype(jnp.bfloat16)

    def exchange(self, step):
        for f in range(len(self.flows)):
            shard = self.shard(f, -step)
            self.stage[self.land_rows(f, shard)] = self.total[self.rows(f, 1 - self.core, shard)].astype(jnp.bfloat16)
            self.core_copy(f, shard).start()

    def of(self, lane):
        return [f for f in range(len(self.flows)) if lane is None or self.flows[f][1] == lane]

    def towards(self, step, lane=None, first=False):
        for f in self.of(lane):
            shard = self.shard(f, step)
            self.core_copy(f, shard).wait_recv()
            if first:
                self.add(f, shard, None)
            else:
                self.ring_copy(f, step - 1, shard).wait_recv()
                self.add(f, shard, step - 1)
            self.ring_copy(f, step, shard).start()

    def back(self, step, lane=None):
        for f in self.of(lane):
            shard = self.shard(f, self.nodes - 1 + step)
            self.back_copy(f, step - 1, shard).wait_recv()
            self.back_copy(f, step, shard).start()
            self.over_copy(f, shard).start()

    def own(self, lane=None):
        for f in self.of(lane):
            shard = self.shard(f, self.nodes - 1)
            self.core_copy(f, shard).wait_recv()
            self.ring_copy(f, self.nodes - 2, shard).wait_recv()
            self.add(f, shard, self.nodes - 2)
            self.back_copy(f, None, shard).start()
            self.over_copy(f, shard, True).start()
            self.keep_copy(f, shard).start()

    def arrive(self, lane=None):
        for f in self.of(lane):
            shard = self.shard(f, 2 * self.nodes - 2)
            self.back_copy(f, self.nodes - 2, shard).wait_recv()
            self.over_copy(f, shard).start()

    def settle(self):
        def crossed(step, carry):
            for f in range(len(self.flows)):
                self.core_copy(f, step).wait_send()
                self.over_copy(f, step).wait()
            return carry

        def rounded(step, carry):
            for f in range(len(self.flows)):
                self.ring_copy(f, step, 0).wait_send()
                self.back_copy(f, step, 0).wait_send()
            return carry

        lax.fori_loop(0, self.nodes, crossed, 0)
        lax.fori_loop(0, self.nodes - 1, rounded, 0)
        for f in range(len(self.flows)):
            self.keep_copy(f, 0).wait()


def run_rings(rings, small_sum):
    ahead, behind = rings
    nodes, lanes = ahead.nodes, ahead.lanes

    def each(method, *step):
        getattr(ahead, method)(*step, 0)
        getattr(behind, method)(*step)
        for lane in range(1, lanes):
            getattr(ahead, method)(*step, lane)

    ahead.exchange(3)
    for lane in range(lanes):
        ahead.towards(1, lane)
    small_sum.step(0)
    for step in (2, 3):
        ahead.exchange(step + 2)
        behind.exchange(2 * step - 2)
        behind.exchange(2 * step - 1)
        ahead.towards(step, 0)
        behind.towards(2 * step - 4, first=step == 2)
        for lane in range(1, lanes):
            ahead.towards(step, lane)
        behind.towards(2 * step - 3)

    def towards(step, carry):
        ahead.exchange(step + 2)
        behind.exchange(step + 2)
        each("towards", step)
        return carry

    lax.fori_loop(4, nodes - 2, towards, 0)
    each("towards", nodes - 2)
    each("own")
    small_sum.step(1)
    at = 1
    for k in range(2, small_sum.steps):
        if at < nodes - 1:
            each("back", at)
            at += 1
        small_sum.step(k)

    def back(step, carry):
        each("back", step)
        return carry

    lax.fori_loop(at, nodes - 1, back, 0)
    each("arrive")
    ahead.settle()
    behind.settle()
    small_sum.settle()


class SmallSum:
    def __init__(self, ring, small, land, out, send_sem, recv_sem, other_section):
        self.peers, self.small, self.land, self.out = ring.peers + [other_section], small, land, out
        self.sems = (send_sem, recv_sem)
        self.remote = ring.remote
        self.steps = len(self.peers) + 1

    def held(self, k):
        return self.small if k == 0 else self.land.at[2 * k - 1]

    def copy(self, k):
        count = self.small.shape[0]
        target = self.out.at[pl.ds(count, count)] if k == len(self.peers) - 1 else self.land.at[2 * k]
        return self.remote(self.held(k), target, self.sems, k, self.peers[k])

    def step(self, k):
        last = len(self.peers) - 1
        if 0 < k:
            self.copy(k - 1).wait_recv()
        if 0 < k <= last:
            self.land[2 * k - 1] = self.held(k - 1)[...] + self.land[2 * k - 2]
        if k <= last:
            self.copy(k).start()
        if k == last:
            self.out[pl.ds(0, self.small.shape[0])] = self.held(k)[...]

    def settle(self):
        for k in range(len(self.peers)):
            self.copy(k).wait_send()


def finish_kernel(
    base, given, big, small, result, grad_in, grad_conv, grad_out, first_gain, first_shift, in_bias, second_gain,
    second_shift, conv_bias, third_gain, third_shift, out_bias, scores, counts,
    passed, held, wide, pass_sem, load_sem, store_sem,
):
    hidden = held.shape[2]
    blocks = held.shape[0]
    ends = grad_in.shape[1] // hidden
    first = pltpu.make_async_copy(given, passed, pass_sem.at[0])
    second = pltpu.make_async_copy(passed, result, pass_sem.at[1])

    def load(b):
        start = b * hidden if b < blocks - ends else base + (b - blocks + ends) * hidden
        return pltpu.make_async_copy(big.at[pl.ds(start, hidden)], held.at[b], load_sem.at[b])

    def store(b):
        if b < KERNEL:
            target = grad_conv.at[0, b]
        elif b < blocks - ends:
            target = grad_out.at[0, :, pl.ds((b - KERNEL) * hidden, hidden)]
        else:
            target = grad_in.at[0, pl.ds((b - blocks + ends) * hidden, hidden)]
        return pltpu.make_async_copy(wide.at[b], target, store_sem.at[b])

    for b in range(LOADS_AHEAD):
        load(b).start()
    first.start()
    first_gain[...] = small[0:1]
    first_shift[...] = small[1:2]
    out_bias[...] = small[2:3]
    for i, ref in enumerate((in_bias, second_gain, second_shift, conv_bias, third_gain, third_shift)):
        ref[...] = small[3 + i // 2 : 4 + i // 2, (i % 2) * hidden : (i % 2 + 1) * hidden]
    hits = small[6:7, 0:VOCAB] + small[14:15, 0:VOCAB]
    tally = small[7:8, 0:VOCAB] + small[15:16, 0:VOCAB]
    scores[...] = hits / jnp.maximum(tally, 1.0)
    counts[...] = tally.astype(jnp.int32)
    for b in range(blocks):
        load(b).wait()
        if b + LOADS_AHEAD < blocks:
            load(b + LOADS_AHEAD).start()
        wide[b] = held[b].astype(jnp.float32)
        store(b).start()
        if b == 1:
            first.wait()
            second.start()
    for b in range(blocks):
        store(b).wait()
    second.wait()


def finish(given, big, small, width, base):
    hidden = big.shape[1]
    blocks = 2 * width // hidden + KERNEL
    full = jnp.float32
    shapes = [(1, width, hidden), (1, KERNEL, hidden, hidden), (1, hidden, width), (1, width), (1, width)]
    shapes += [(1, hidden)] * 6 + [(1, width), (1, VOCAB)]
    out = [jax.ShapeDtypeStruct(given.shape, given.dtype)]
    out += [jax.ShapeDtypeStruct(shape, full) for shape in shapes] + [jax.ShapeDtypeStruct((1, VOCAB), jnp.int32)]
    return pl.pallas_call(
        functools.partial(finish_kernel, base),
        out_shape=out,
        in_specs=[pl.BlockSpec(memory_space=pltpu.HBM)] * 2 + [pl.BlockSpec(memory_space=pltpu.VMEM)],
        out_specs=[pl.BlockSpec(memory_space=pltpu.HBM)] * 4 + [pl.BlockSpec(memory_space=pltpu.VMEM)] * (len(out) - 4),
        scratch_shapes=[
            pltpu.VMEM(given.shape, given.dtype),
            pltpu.VMEM((blocks, hidden, hidden), big.dtype),
            pltpu.VMEM((blocks, hidden, hidden), full),
            pltpu.SemaphoreType.DMA((2,)),
            pltpu.SemaphoreType.DMA((blocks,)),
            pltpu.SemaphoreType.DMA((blocks,)),
        ],
        compiler_params=pltpu.CompilerParams(vmem_limit_bytes=VMEM_BYTES),
    )(given, big, small)


def shards(
    boundary, lengths, masked, residues, readout,
    first_gain, first_shift, in_weight, in_bias, second_gain, second_shift, conv_weight, conv_bias,
    third_gain, third_shift, out_weight, out_bias,
):
    ny, nz = lax.axis_size("seq") // 2, lax.axis_size("dp")
    width, hidden = in_weight.shape[1], in_weight.shape[2]
    given, big, small = run_blocks(
        (
            boundary, lengths, masked, residues, readout.T,
            first_gain, first_shift, in_weight, in_bias, second_gain, second_shift, conv_weight, conv_bias,
            third_gain, third_shift, out_weight, out_bias,
        ),
        ny,
        nz,
    )
    (
        boundary_out, grad_in_weight, grad_conv_weight, grad_out_weight, grad_first_gain, grad_first_shift, grad_in_bias,
        grad_second_gain, grad_second_shift, grad_conv_bias, grad_third_gain, grad_third_shift, grad_out_bias,
        scores, counts,
    ) = finish(given, big, small, width, ring_plan(width, hidden, ny * nz)[0][1][1])
    return (
        boundary_out,
        grad_first_gain,
        grad_first_shift,
        grad_in_weight,
        grad_in_bias,
        grad_second_gain,
        grad_second_shift,
        grad_conv_weight,
        grad_conv_bias,
        grad_third_gain,
        grad_third_shift,
        grad_out_weight,
        grad_out_bias,
        scores[0],
        counts[0],
    )


def solution(mesh):
    in_specs = (
        P("section", "dp", "seq", None),
        P("dp", None),
        P("dp", "seq"),
        P("dp", "seq"),
        P(),
        P("section", None),
        P("section", None),
        P("section", None, None),
        P("section", None),
        P("section", None),
        P("section", None),
        P("section", None, None, None),
        P("section", None),
        P("section", None),
        P("section", None),
        P("section", None, None),
        P("section", None),
    )
    out_specs = (
        P("section", "dp", "seq", None),
        P("section", None),
        P("section", None),
        P("section", None, None),
        P("section", None),
        P("section", None),
        P("section", None),
        P("section", None, None, None),
        P("section", None),
        P("section", None),
        P("section", None),
        P("section", None, None),
        P("section", None),
        P(),
        P(),
    )
    return jax.shard_map(shards, mesh=mesh, in_specs=in_specs, out_specs=out_specs, check_vma=False)
```

profile of v0, /device:TPU:0, one launch (start us, length us, event | category | flops | bytes accessed | tf_op | source)
XLA Modules:
  0.0 205.4 jit_solution(2446656640402520027)
XLA Ops:
  0.7 193.7 %shard_map.280 = (bf16[1,4,256,1280]{3,2,1,0:T(8,128)(2,1)}, bf16[5888,640]{1,0:T(8,128)(2,1)}, f32[16,1280]{1,0:T(8,128)}) custom-call(bf16[1,4,256,1280]{3,2,1,0:T(8,128)(2,1)} %boundary.1, s32[4,4]{1,0:T(4,128)} %lengths.1, s32[4,256]{1,0:T(4,128)} %masked.1, s32[4,256]{1,0:T(4,128)} %residues.1, bf16[30,1280]{1,0:T(8,128)(2,1)} %bitcast.3, ...), custom_call_target="tpu_custom_call" | custom-call | tf_op jit(solution)/shard_map/pallas_call | solution.py:584
  194.3 10.9 %shard_map.281 = (bf16[1,4,256,1280]{3,2,1,0:T(8,128)(2,1)}, f32[1,1280,640]{2,1,0:T(8,128)}, f32[1,5,640,640]{3,2,1,0:T(8,128)}, f32[1,640,1280]{2,1,0:T(8,128)...) custom-call(bf16[1,4,256,1280]{3,2,1,0:T(8,128)(2,1)} %get-tuple-ele, ...), custom_call_target="tpu_custom_call" | custom-call | tf_op jit(solution)/shard_map/pallas_call | solution.py:951
where the time goes:
time: 206 us; the launch traced here: 205 us
  Pallas kernels  205 us (100%)
    pallas_call x1, Pallas kernels, run_blocks(): pl.pallas_call(functools.partial(blocks_kernel, edge, plan), out_shape=(j...  194 us
    pallas_call x1, Pallas kernels, finish(): pl.pallas_call(functools.partial(finish_kernel, base), out_shape=out, in_...  10.9 us

commit v1 on v0

--- a/solution.py
+++ b/solution.py
@@ -18,7 +18,6 @@
 
 MESH = pl.DeviceIdType.MESH
 LANES = 2
-LOADS_AHEAD = 4
 VMEM_BYTES = 64 << 20
 
 
@@ -77,14 +76,16 @@
 
 def blocks_kernel(
     edge, plan,
-    boundary, lengths, masked, residues, readout,
-    first_gain, first_shift, in_weight, in_bias, second_gain, second_shift, conv_weight, conv_bias,
-    third_gain, third_shift, out_weight, out_bias,
+    boundary, lengths, masked_in, residues_in, readout_in,
+    first_gain_in, first_shift_in, in_weight, in_bias_in, second_gain_in, second_shift_in, conv_weight, conv_bias_in,
+    third_gain_in, third_shift_in, out_weight, out_bias_in,
     result, big, small_out,
+    masked, residues, readout, first_gain, first_shift, in_bias, second_gain, second_shift, conv_bias,
+    third_gain, third_shift, out_bias,
     buf, w_in, w_conv, w_out, total, hat1, slope1, act1, taps, back_taps,
     hat2, slope2, hat3, slope3, act3, rim_left, rim_right, near, masks,
     sums_wide, sums, hits, tally, core_land, small, small_land,
-    load_sem, weight_sem, result_sem, hand_send, hand_recv, rim_send, rim_recv, small_send, small_recv, *ring_refs,
+    load_sem, weight_sem, result_sem, hand_send, hand_recv, rim_send, rim_recv, small_send, small_recv, input_sem, *ring_refs,
 ):
     grad1, grad2 = hat2, hat3
     section = lax.axis_index("section")
@@ -107,8 +108,19 @@
         pltpu.make_async_copy(source.at[0], target, weight_sem.at[i])
         for i, (source, target) in enumerate(((in_weight, w_in), (conv_weight, w_conv), (out_weight, w_out)))
     ]
+    input_loads = [
+        pltpu.make_async_copy(source, target, input_sem.at[i])
+        for i, (source, target) in enumerate((
+            (first_gain_in, first_gain), (first_shift_in, first_shift), (in_bias_in, in_bias),
+            (second_gain_in, second_gain), (second_shift_in, second_shift), (conv_bias_in, conv_bias),
+            (third_gain_in, third_gain), (third_shift_in, third_shift), (out_bias_in, out_bias),
+            (masked_in, masked), (residues_in, residues), (readout_in, readout),
+        ))
+    ]
     load(0).start()
     weight_loads[0].start()
+    for copy in input_loads:
+        copy.start()
 
     def partner():
         return (1 - section, seq, dp)
@@ -314,19 +326,21 @@
         grad2[m, block] = low
         sums[3] += fold(low.astype(jnp.float32))
 
-    def back_middle_tap(m):
-        return dot_nt(grad2[m], w_conv[KERNEL // 2])
-
-    def back_rear(m, grad, between=None):
+    def back_middle_tap(m, piece=None):
+        block = slice(0, positions) if piece is None else slice(piece[0], piece[0] + piece[1])
+        return dot_nt(grad2[m, block], w_conv[KERNEL // 2])
+
+    def back_rear(m, piece, grad, between=None):
+        block = slice(piece[0], piece[0] + piece[1])
         for k in range(KERNEL):
             if k != KERNEL // 2:
-                grad = grad + dot_nt(back_taps[k - (k > KERNEL // 2)], w_conv[KERNEL - 1 - k])
+                grad = grad + dot_nt(back_taps[k - (k > KERNEL // 2), block], w_conv[KERNEL - 1 - k])
         if between is not None:
             between()
         low = act_backward(
-            grad, hat2[m], slope2[m], masks[m, :, 9:10], second_gain[...], sums.at[1], sums.at[2]
+            grad, hat2[m, block], slope2[m, block], masks[m, block, 9:10], second_gain[...], sums.at[1], sums.at[2]
         ).astype(jnp.bfloat16)
-        grad1[m] = low
+        grad1[m, block] = low
         sums[0] += fold(low.astype(jnp.float32))
 
     def back_last(m, piece):
@@ -361,12 +375,16 @@
         rings[0].exchange(2)
         rings[0].towards(0, 0, True)
 
+    def other_lanes():
+        for lane in range(1, rings[0].lanes):
+            rings[0].towards(0, lane, True)
+
     def step(i, carry):
         fronts = i < rows
         m_start = jnp.where(leading, i - rows, i)
         m_end = m_start - 1
-        m_sum = i - rows
-        final = i == 2 * rows
+        m_sum = jnp.where(leading, i - rows, i - rows + 1)
+        final = m_sum == rows
 
         def on(m):
             return (m >= 0) & (m < rows)
@@ -380,90 +398,36 @@
             weight_loads[0].wait()
             for copy in weight_loads[1:]:
                 copy.start()
+            for copy in input_loads:
+                copy.wait()
 
         @pl.when(leading & fronts)
         def _():
             load(i).wait()
 
+        @pl.when(leading & fronts)
+        def _():
+            front(i, whole[0])
+
         @pl.when(i == 0)
         def _():
+            weight_loads[1].wait()
+            weight_loads[2].wait()
             for m in range(1, rows):
                 load(m).start()
 
-        @pl.when(trailing & (i < last))
-        def _():
-            for part in range(3):
-                hand(buf, i, part).wait_recv()
-
-        @pl.when(fronts & (leading | (i < last)))
-        def _():
-            front(i, whole[0])
-
-        @pl.when(i == 0)
-        def _():
-            pl.semaphore_wait(barrier, greeted)
-
-        @pl.when(leading & fronts)
-        def _():
-            begin(near_copies(0, i))
-
-        @pl.when(trailing & (i < last))
-        def _():
-            begin(far_copies(0, i, 0, whole))
-
-        @pl.when(trailing & (i == last))
-        def _():
-            for part in range(3):
-                hand(buf, last, part).wait_recv()
-                front(last, thirds[part])
-                begin(far_copies(0, last, part, thirds))
-
-        @pl.when(i == 0)
-        def _():
-            weight_loads[1].wait()
-            weight_loads[2].wait()
-
-        @pl.when(on(m_end))
-        def _():
-            grad = back_middle_tap(m_end)
-
-            @pl.when(leading)
-            def _():
-                gather_near(1, m_end, grad2[m_end], store_back, False)
-                end(near_copies(1, m_end))
-                gather_near(1, m_end, grad2[m_end], store_back, True)
-
-            @pl.when(trailing)
-            def _():
-                for part in range(2):
-                    end(far_copies(1, m_end, part, parts))
-                gather_far(1, m_end, grad2[m_end], store_back)
-
-            back_rear(m_end, grad, lambda: pl.when(final)(first_lane))
-            for part in range(2):
-                back_last(m_end, parts[part])
-                pl.when(trailing)(hand(hat1, m_end, part).start)
-            pl.when(leading)(give(hat1, m_end).start)
-
-        @pl.when(trailing & final)
-        def _():
-            first_lane()
-
-        @pl.when(on(m_sum - 1))
-        def _():
-            weights_in(m_sum - 1)
-
-        @pl.when(final)
-        def _():
-            for lane in range(1, rings[0].lanes):
-                rings[0].towards(0, lane, True)
-            rings[1].exchange(0)
-            rings[1].exchange(1)
-
         @pl.when(leading & fronts)
         def _():
             gather_near(0, i, taps[tap_rows(i, KERNEL // 2)], store_tap(i), False)
             rear(i, thirds[0], middle_tap(i, thirds[0]))
+
+        @pl.when(i == 0)
+        def _():
+            pl.semaphore_wait(barrier, greeted)
+
+        @pl.when(leading & fronts)
+        def _():
+            begin(near_copies(0, i))
             hand(buf, i, 0).start()
             end(near_copies(0, i))
             gather_near(0, i, taps[tap_rows(i, KERNEL // 2)], store_tap(i), True)
@@ -471,6 +435,51 @@
                 rear(i, thirds[part], middle_tap(i, thirds[part]))
                 hand(buf, i, part).start()
 
+        @pl.when(trailing & fronts)
+        def _():
+            for part in range(3):
+                hand(buf, i, part).wait_recv()
+                front(i, thirds[part])
+                begin(far_copies(0, i, part, thirds))
+
+        @pl.when(leading & on(m_end))
+        def _():
+            grad = back_middle_tap(m_end)
+            gather_near(1, m_end, grad2[m_end], store_back, False)
+            end(near_copies(1, m_end))
+            gather_near(1, m_end, grad2[m_end], store_back, True)
+            back_rear(m_end, whole[0], grad, lambda: pl.when(final)(first_lane))
+            back_last(m_end, whole[0])
+            give(hat1, m_end).start()
+            pl.when(final)(other_lanes)
+
+        @pl.when(trailing & on(m_end))
+        def _():
+            grads = [back_middle_tap(m_end, piece) for piece in parts]
+            for part in range(2):
+                end(far_copies(1, m_end, part, parts))
+            gather_far(1, m_end, grad2[m_end], store_back)
+            for part in range(2):
+                back_rear(m_end, parts[part], grads[part])
+                back_last(m_end, parts[part])
+                hand(hat1, m_end, part).start()
+
+        @pl.when(trailing & final)
+        def _():
+            first_lane()
+            other_lanes()
+
+        @pl.when(on(m_sum - 1))
+        def _():
+            weights_in(m_sum - 1)
+
+        @pl.when(final)
+        def _():
+            rings[0].towards(1, 0)
+            rings[0].exchange(3)
+            rings[1].exchange(0)
+            rings[1].exchange(1)
+
         @pl.when((leading & (i == 2)) | (trailing & (i == 0)))
         def _():
             total[...] = jnp.zeros_like(total)
@@ -483,15 +492,8 @@
         def _():
             pre = middle_tap(i, whole[0])
 
-            @pl.when(i < last)
-            def _():
-                end(far_copies(0, i, 0, whole))
-
-            @pl.when(i == last)
-            def _():
-                for part in range(3):
-                    end(far_copies(0, last, part, thirds))
-
+            for part in range(3):
+                end(far_copies(0, i, part, thirds))
             gather_far(0, i, taps[tap_rows(i, KERNEL // 2)], store_tap(i))
             rear(i, whole[0], pre)
             give(buf, i).start()
@@ -520,7 +522,7 @@
             weights_out(m_sum)
             weights_conv(m_sum)
 
-        @pl.when(i == 2 * rows - 1)
+        @pl.when(m_sum == last)
         def _():
             rings[0].exchange(0)
             rings[0].exchange(1)
@@ -529,18 +531,20 @@
 
     lax.fori_loop(0, 2 * rows + 1, step, 0)
 
-    for i in range(3):
-        small[i : i + 1, :] = jnp.sum(sums_wide[i], axis=0, keepdims=True)
-    for i in range(6):
-        small[3 + i // 2 : 4 + i // 2, (i % 2) * hidden : (i % 2 + 1) * hidden] = jnp.sum(sums[i], axis=0, keepdims=True)
-    small[6:8, :] = jnp.zeros((2, small.shape[1]), jnp.float32)
-    ones = jnp.ones((8, positions), jnp.float32)
-    for i, counted in ((6, hits), (7, tally)):
-        row = lax.dot_general(
-            ones, counted[...], (((1,), (1,)), ((), ())), precision=lax.Precision.HIGHEST,
-            preferred_element_type=jnp.float32)
-        small[i : i + 1, 0 : counted.shape[0]] = row[0:1]
-    run_rings(rings, SmallSum(rings[0], small, small_land, small_out, small_send, small_recv, partner()))
+    def fill_small():
+        for i in range(3):
+            small[i : i + 1, :] = jnp.sum(sums_wide[i], axis=0, keepdims=True)
+        for i in range(6):
+            small[3 + i // 2 : 4 + i // 2, (i % 2) * hidden : (i % 2 + 1) * hidden] = jnp.sum(sums[i], axis=0, keepdims=True)
+        small[6:8, :] = jnp.zeros((2, small.shape[1]), jnp.float32)
+        ones = jnp.ones((8, positions), jnp.float32)
+        for i, counted in ((6, hits), (7, tally)):
+            row = lax.dot_general(
+                ones, counted[...], (((1,), (1,)), ((), ())), precision=lax.Precision.HIGHEST,
+                preferred_element_type=jnp.float32)
+            small[i : i + 1, 0 : counted.shape[0]] = row[0:1]
+
+    run_rings(rings, fill_small, SmallSum(rings[0], small, small_land, small_out, small_send, small_recv, partner()))
     for m in range(rows):
         @pl.when(leading)
         def _():
@@ -578,9 +582,8 @@
     wide_rows = pltpu.VMEM((rows, positions, width), low)
     thin_rows = pltpu.VMEM((rows, positions, hidden), low)
     plan, half = ring_plan(width, hidden, nodes)
-    where = [pltpu.HBM, pltpu.SMEM] + [pltpu.VMEM] * 15
-    for i in (7, 11, 15):
-        where[i] = pltpu.HBM
+    where = [pltpu.HBM, pltpu.SMEM] + [pltpu.HBM] * 15
+    smalls = [pltpu.VMEM(args[i].shape, args[i].dtype) for i in (2, 3, 4, 5, 6, 8, 9, 10, 12, 13, 14, 16)]
     return pl.pallas_call(
         functools.partial(blocks_kernel, edge, plan),
         out_shape=(
@@ -590,7 +593,7 @@
         ),
         in_specs=[pl.BlockSpec(memory_space=space) for space in where],
         out_specs=[pl.BlockSpec(memory_space=space) for space in (pltpu.HBM, pltpu.HBM, pltpu.VMEM)],
-        scratch_shapes=[
+        scratch_shapes=smalls + [
             pltpu.VMEM((2 * rows, positions, width), low),
             pltpu.VMEM((width, hidden), low),
             pltpu.VMEM((KERNEL, hidden, hidden), low),
@@ -620,6 +623,7 @@
             pltpu.SemaphoreType.DMA((2 * rows, 6 * reach)),
             pltpu.SemaphoreType.DMA((doublings + 1,)),
             pltpu.SemaphoreType.DMA((doublings + 1,)),
+            pltpu.SemaphoreType.DMA((len(smalls),)),
         ]
         + [scratch for sizes, _, _ in plan for scratch in ring_scratch(sizes, nodes, hidden)],
         compiler_params=pltpu.CompilerParams(
@@ -807,7 +811,7 @@
             self.keep_copy(f, 0).wait()
 
 
-def run_rings(rings, small_sum):
+def run_rings(rings, fill_small, small_sum):
     ahead, behind = rings
     nodes, lanes = ahead.nodes, ahead.lanes
 
@@ -817,10 +821,8 @@
         for lane in range(1, lanes):
             getattr(ahead, method)(*step, lane)
 
-    ahead.exchange(3)
-    for lane in range(lanes):
+    for lane in range(1, lanes):
         ahead.towards(1, lane)
-    small_sum.step(0)
     for step in (2, 3):
         ahead.exchange(step + 2)
         behind.exchange(2 * step - 2)
@@ -830,6 +832,9 @@
         for lane in range(1, lanes):
             ahead.towards(step, lane)
         behind.towards(2 * step - 3)
+
+    fill_small()
+    small_sum.step(0)
 
     def towards(step, carry):
         ahead.exchange(step + 2)
@@ -891,15 +896,16 @@
 
 
 def finish_kernel(
-    base, given, big, small, result, grad_in, grad_conv, grad_out, first_gain, first_shift, in_bias, second_gain,
+    base, given, big, small_in, result, grad_in, grad_conv, grad_out, first_gain, first_shift, in_bias, second_gain,
     second_shift, conv_bias, third_gain, third_shift, out_bias, scores, counts,
-    passed, held, wide, pass_sem, load_sem, store_sem,
+    small, passed, held, wide, rate, count, pass_sem, load_sem, store_sem, small_sem,
 ):
     hidden = held.shape[2]
     blocks = held.shape[0]
     ends = grad_in.shape[1] // hidden
-    first = pltpu.make_async_copy(given, passed, pass_sem.at[0])
-    second = pltpu.make_async_copy(passed, result, pass_sem.at[1])
+    small_load = pltpu.make_async_copy(small_in, small, pass_sem.at[0])
+    first = pltpu.make_async_copy(given, passed, pass_sem.at[1])
+    second = pltpu.make_async_copy(passed, result, pass_sem.at[2])
 
     def load(b):
         start = b * hidden if b < blocks - ends else base + (b - blocks + ends) * hidden
@@ -914,29 +920,37 @@
             target = grad_in.at[0, pl.ds((b - blocks + ends) * hidden, hidden)]
         return pltpu.make_async_copy(wide.at[b], target, store_sem.at[b])
 
-    for b in range(LOADS_AHEAD):
+    load(0).start()
+    small_load.start()
+    for b in range(1, blocks):
         load(b).start()
     first.start()
-    first_gain[...] = small[0:1]
-    first_shift[...] = small[1:2]
-    out_bias[...] = small[2:3]
-    for i, ref in enumerate((in_bias, second_gain, second_shift, conv_bias, third_gain, third_shift)):
-        ref[...] = small[3 + i // 2 : 4 + i // 2, (i % 2) * hidden : (i % 2 + 1) * hidden]
-    hits = small[6:7, 0:VOCAB] + small[14:15, 0:VOCAB]
-    tally = small[7:8, 0:VOCAB] + small[15:16, 0:VOCAB]
-    scores[...] = hits / jnp.maximum(tally, 1.0)
-    counts[...] = tally.astype(jnp.int32)
     for b in range(blocks):
         load(b).wait()
-        if b + LOADS_AHEAD < blocks:
-            load(b + LOADS_AHEAD).start()
         wide[b] = held[b].astype(jnp.float32)
         store(b).start()
-        if b == 1:
-            first.wait()
-            second.start()
+        if b == 0:
+            small_load.wait()
+            hits = small[6:7, 0:VOCAB] + small[14:15, 0:VOCAB]
+            tally = small[7:8, 0:VOCAB] + small[15:16, 0:VOCAB]
+            rate[...] = hits / jnp.maximum(tally, 1.0)
+            count[...] = tally.astype(jnp.int32)
+            pieces = [(small.at[pl.ds(i, 1)], ref) for i, ref in enumerate((first_gain, first_shift, out_bias))]
+            thin = (in_bias, second_gain, second_shift, conv_bias, third_gain, third_shift)
+            for i, ref in enumerate(thin):
+                pieces.append((small.at[pl.ds(3 + i // 2, 1), pl.ds(i % 2 * hidden, hidden)], ref))
+            pieces += [(rate, scores), (count, counts)]
+            small_stores = [
+                pltpu.make_async_copy(source, target, small_sem.at[i]) for i, (source, target) in enumerate(pieces)
+            ]
+            for copy in small_stores:
+                copy.start()
+    first.wait()
+    second.start()
     for b in range(blocks):
         store(b).wait()
+    for copy in small_stores:
+        copy.wait()
     second.wait()
 
 
@@ -951,15 +965,19 @@
     return pl.pallas_call(
         functools.partial(finish_kernel, base),
         out_shape=out,
-        in_specs=[pl.BlockSpec(memory_space=pltpu.HBM)] * 2 + [pl.BlockSpec(memory_space=pltpu.VMEM)],
-        out_specs=[pl.BlockSpec(memory_space=pltpu.HBM)] * 4 + [pl.BlockSpec(memory_space=pltpu.VMEM)] * (len(out) - 4),
+        in_specs=[pl.BlockSpec(memory_space=pltpu.HBM)] * 3,
+        out_specs=[pl.BlockSpec(memory_space=pltpu.HBM)] * len(out),
         scratch_shapes=[
+            pltpu.VMEM(small.shape, full),
             pltpu.VMEM(given.shape, given.dtype),
             pltpu.VMEM((blocks, hidden, hidden), big.dtype),
             pltpu.VMEM((blocks, hidden, hidden), full),
-            pltpu.SemaphoreType.DMA((2,)),
+            pltpu.VMEM((1, VOCAB), full),
+            pltpu.VMEM((1, VOCAB), jnp.int32),
+            pltpu.SemaphoreType.DMA((3,)),
             pltpu.SemaphoreType.DMA((blocks,)),
             pltpu.SemaphoreType.DMA((blocks,)),
+            pltpu.SemaphoreType.DMA((11,)),
         ],
         compiler_params=pltpu.CompilerParams(vmem_limit_bytes=VMEM_BYTES),
     )(given, big, small)

time: 206 us -> 201 us (0.976)
  Pallas kernels: 205 us -> 200 us
    pallas_call x1, Pallas kernels: 194 us -> 191 us  [run_blocks(): pl.pallas_call(functools.partial(blocks_kernel, edge, plan), out_shape=(j...]
where the time goes in v1:
time: 201 us
  Pallas kernels  200 us (100%)
    pallas_call x1, Pallas kernels, run_blocks(): pl.pallas_call(functools.partial(blocks_kernel, edge, plan), out_shape=(j...  191 us
    pallas_call x1, Pallas kernels, finish(): pl.pallas_call(functools.partial(finish_kernel, base), out_shape=out, in_...  9.18 us

profile of v1, /device:TPU:0, one launch (start us, length us, event | category | flops | bytes accessed | tf_op | source)
XLA Modules:
  0.0 200.8 jit_solution(17038317389376442089)
XLA Ops:
  0.7 190.8 %shard_map.280 = (bf16[1,4,256,1280]{3,2,1,0:T(8,128)(2,1)}, bf16[5888,640]{1,0:T(8,128)(2,1)}, f32[16,1280]{1,0:T(8,128)}) custom-call(bf16[1,4,256,1280]{3,2,1,0:T(8,128)(2,1)} %boundary.1, s32[4,4]{1,0:T(4,128)} %lengths.1, s32[4,256]{1,0:T(4,128)} %masked_in.1, s32[4,256]{1,0:T(4,128)} %residues_in.1, bf16[30,1280]{1,0:T(8,128)(2,1)} %bitcast.3, ...), custom_call_target="tpu_custom_call" | custom-call | tf_op jit(solution)/shard_map/pallas_call | solution.py:587
  191.5 9.2 %shard_map.281 = (bf16[1,4,256,1280]{3,2,1,0:T(8,128)(2,1)}, f32[1,1280,640]{2,1,0:T(8,128)}, f32[1,5,640,640]{3,2,1,0:T(8,128)}, f32[1,640,1280]{2,1,0:T(8,128)...) custom-call(bf16[1,4,256,1280]{3,2,1,0:T(8,128)(2,1)} %get-tuple-ele, ...), custom_call_target="tpu_custom_call" | custom-call | tf_op jit(solution)/shard_map/pallas_call | solution.py:965

commit v2 on v1

--- a/solution.py
+++ b/solution.py
@@ -85,7 +85,8 @@
     buf, w_in, w_conv, w_out, total, hat1, slope1, act1, taps, back_taps,
     hat2, slope2, hat3, slope3, act3, rim_left, rim_right, near, masks,
     sums_wide, sums, hits, tally, core_land, small, small_land,
-    load_sem, weight_sem, result_sem, hand_send, hand_recv, rim_send, rim_recv, small_send, small_recv, input_sem, *ring_refs,
+    load_sem, weight_sem, result_sem, hand_send, hand_recv, rim_send, rim_recv, small_send, small_recv, input_sem,
+    low_land, far_gain, far_shift, gift_send, gift_recv, *ring_refs,
 ):
     grad1, grad2 = hat2, hat3
     section = lax.axis_index("section")
@@ -182,6 +183,58 @@
             send_sem=hand_send.at[m, part], recv_sem=hand_recv.at[m, part],
             device_id=partner(), device_id_type=MESH)
 
+    def low_hand(part):
+        block = pl.ds(*parts[part])
+        return pltpu.make_async_remote_copy(
+            src_ref=grad1.at[last, block], dst_ref=low_land.at[block],
+            send_sem=hand_send.at[last, part], recv_sem=hand_recv.at[last, part],
+            device_id=partner(), device_id_type=MESH)
+
+    core = seq % 2
+    wide_half = buf.shape[2] // 2
+    own_half = pl.ds(pl.multiple_of(core * wide_half, 16), wide_half)
+    other_half = pl.ds(pl.multiple_of((1 - core) * wide_half, 16), wide_half)
+
+    def gift(i):
+        source, target = (
+            (w_in.at[own_half], core_land.at[own_half]),
+            (buf.at[rows + last], buf.at[rows + last]),
+            (first_gain, far_gain),
+            (first_shift, far_shift),
+        )[i]
+        return pltpu.make_async_remote_copy(
+            src_ref=source, dst_ref=target, send_sem=gift_send.at[i], recv_sem=gift_recv.at[i],
+            device_id=partner(), device_id_type=MESH)
+
+    def pass_on(half):
+        return pltpu.make_async_remote_copy(
+            src_ref=core_land.at[half], dst_ref=core_land.at[half],
+            send_sem=gift_send.at[4], recv_sem=gift_recv.at[4],
+            device_id=(section, seq + 1 - 2 * core, dp), device_id_type=MESH)
+
+    def far_norm():
+        for m in (1, 2):
+            for part in range(3):
+                hand(buf, m, part).wait_send()
+        for first, count in parts:
+            block = slice(first, first + count)
+            real = masks[last, block, KERNEL // 2 : KERNEL // 2 + 1]
+            _, hat, slope, inverse = act_forward(
+                buf[last, block].astype(jnp.float32), far_gain[...], far_shift[...], real)
+            buf[1, block] = hat.astype(jnp.bfloat16)
+            buf[2, block] = slope.astype(jnp.bfloat16)
+            masks[last, block, 11:12] = inverse
+
+    def far_last(piece):
+        block = slice(piece[0], piece[0] + piece[1])
+        scale = 1.0 / buf.shape[2]
+        hat = buf[1, block].astype(jnp.float32)
+        grad = dot_nt(low_land[block], core_land[0 : 2 * wide_half]) * buf[2, block].astype(jnp.float32) * far_gain[...]
+        mean = jnp.sum(grad, axis=1, keepdims=True) * scale
+        tilt = jnp.sum(grad * hat, axis=1, keepdims=True) * scale
+        grad = masks[last, block, 11:12] * (grad - mean - hat * tilt)
+        buf[rows + last, block] = (buf[rows + last, block].astype(jnp.float32) + grad).astype(jnp.bfloat16)
+
     def tap_rows(m, k, first=0, count=None):
         start = (m * KERNEL + k) * positions + first
         return pl.ds(pl.multiple_of(start, 16), positions if count is None else count)
@@ -382,9 +435,12 @@
     def step(i, carry):
         fronts = i < rows
         m_start = jnp.where(leading, i - rows, i)
-        m_end = m_start - 1
         m_sum = jnp.where(leading, i - rows, i - rows + 1)
-        final = m_sum == rows
+        put_off = i >= 2 * rows - 1
+        m_end = jnp.where(leading, jnp.where(put_off, i - rows - 2, i - rows - 1), i - 1)
+        ends = trailing | (i != 2 * rows - 1)
+        m_in = jnp.where(leading, m_end, i - rows)
+        final = trailing & (i == 2 * rows - 1)
 
         def on(m):
             return (m >= 0) & (m < rows)
@@ -398,6 +454,8 @@
             weight_loads[0].wait()
             for copy in weight_loads[1:]:
                 copy.start()
+            for m in range(1, rows):
+                load(m).start()
             for copy in input_loads:
                 copy.wait()
 
@@ -405,6 +463,15 @@
         def _():
             load(i).wait()
 
+        @pl.when(trailing & (i == 0))
+        def _():
+            pl.semaphore_wait(barrier, greeted)
+            gift(0).start()
+            for k in (2, 3):
+                gift(k).start()
+            load(last).wait()
+            gift(1).start()
+
         @pl.when(leading & fronts)
         def _():
             front(i, whole[0])
@@ -413,15 +480,13 @@
         def _():
             weight_loads[1].wait()
             weight_loads[2].wait()
-            for m in range(1, rows):
-                load(m).start()
 
         @pl.when(leading & fronts)
         def _():
             gather_near(0, i, taps[tap_rows(i, KERNEL // 2)], store_tap(i), False)
             rear(i, thirds[0], middle_tap(i, thirds[0]))
 
-        @pl.when(i == 0)
+        @pl.when(leading & (i == 0))
         def _():
             pl.semaphore_wait(barrier, greeted)
 
@@ -442,16 +507,42 @@
                 front(i, thirds[part])
                 begin(far_copies(0, i, part, thirds))
 
-        @pl.when(leading & on(m_end))
+        @pl.when(leading & (i == last))
+        def _():
+            gift(0).wait_recv()
+            pass_on(own_half).start()
+
+        @pl.when(leading & (i == rows + 1))
+        def _():
+            for k in range(1, 4):
+                gift(k).wait_recv()
+            far_norm()
+            pass_on(own_half).wait_send()
+            pass_on(other_half).wait_recv()
+
+        @pl.when(leading & on(m_end) & ends)
         def _():
             grad = back_middle_tap(m_end)
             gather_near(1, m_end, grad2[m_end], store_back, False)
-            end(near_copies(1, m_end))
+
+            @pl.when(m_end < last - 1)
+            def _():
+                end(near_copies(1, m_end))
+
             gather_near(1, m_end, grad2[m_end], store_back, True)
-            back_rear(m_end, whole[0], grad, lambda: pl.when(final)(first_lane))
+
+            def lanes_between():
+                pl.when(i == 2 * rows)(first_lane)
+
+                @pl.when(i == 2 * rows + 1)
+                def _():
+                    rings[0].towards(1, 0)
+                    rings[0].exchange(3)
+
+            back_rear(m_end, whole[0], grad, lanes_between)
             back_last(m_end, whole[0])
             give(hat1, m_end).start()
-            pl.when(final)(other_lanes)
+            pl.when(i == 2 * rows)(other_lanes)
 
         @pl.when(trailing & on(m_end))
         def _():
@@ -461,22 +552,26 @@
             gather_far(1, m_end, grad2[m_end], store_back)
             for part in range(2):
                 back_rear(m_end, parts[part], grads[part])
+                pl.when(m_end == last)(low_hand(part).start)
                 back_last(m_end, parts[part])
-                hand(hat1, m_end, part).start()
-
-        @pl.when(trailing & final)
+                pl.when(m_end < last)(hand(hat1, m_end, part).start)
+
+        @pl.when(final)
         def _():
             first_lane()
             other_lanes()
 
-        @pl.when(on(m_sum - 1))
-        def _():
-            weights_in(m_sum - 1)
+        @pl.when(on(m_in) & ends)
+        def _():
+            weights_in(m_in)
 
         @pl.when(final)
         def _():
             rings[0].towards(1, 0)
             rings[0].exchange(3)
+
+        @pl.when(final | (leading & (i == 2 * rows + 1)))
+        def _():
             rings[1].exchange(0)
             rings[1].exchange(1)
 
@@ -500,15 +595,25 @@
 
         @pl.when(on(m_start))
         def _():
-            pl.when(trailing)(load(m_start).wait)
+            pl.when(trailing & (m_start < last))(load(m_start).wait)
             for part in range(2):
-                pl.when(leading)(hand(hat1, m_start, part).wait_recv)
+                pl.when(leading & (m_start < last))(hand(hat1, m_start, part).wait_recv)
+
+                @pl.when(leading & (m_start == last))
+                def _():
+                    low_hand(part).wait_recv()
+                    far_last(parts[part])
+
                 back_front(m_start, parts[part])
 
                 @pl.when(trailing)
                 def _():
                     begin(far_copies(1, m_start, part, parts))
 
+            @pl.when(leading & (m_start == last))
+            def _():
+                end(near_copies(1, last - 1))
+
             @pl.when(leading)
             def _():
                 begin(near_copies(1, m_start))
@@ -522,6 +627,10 @@
             weights_out(m_sum)
             weights_conv(m_sum)
 
+        @pl.when(leading & (m_sum == last))
+        def _():
+            end(near_copies(1, last))
+
         @pl.when(m_sum == last)
         def _():
             rings[0].exchange(0)
@@ -529,7 +638,7 @@
 
         return carry
 
-    lax.fori_loop(0, 2 * rows + 1, step, 0)
+    lax.fori_loop(0, 2 * rows + 2, step, 0)
 
     def fill_small():
         for i in range(3):
@@ -548,15 +657,21 @@
     for m in range(rows):
         @pl.when(leading)
         def _():
-            for part in range(3):
-                hand(buf, m, part).wait_send()
+            if m not in (1, 2):
+                for part in range(3):
+                    hand(buf, m, part).wait_send()
             give(hat1, m).wait()
 
         @pl.when(trailing)
         def _():
             for part in range(2):
-                hand(hat1, m, part).wait_send()
+                (hand(hat1, m, part) if m < last else low_hand(part)).wait_send()
             give(buf, m).wait()
+
+    @pl.when(trailing)
+    def _():
+        for k in range(4):
+            gift(k).wait_send()
 
 
 def ring_plan(width, hidden, nodes):
@@ -624,6 +739,11 @@
             pltpu.SemaphoreType.DMA((doublings + 1,)),
             pltpu.SemaphoreType.DMA((doublings + 1,)),
             pltpu.SemaphoreType.DMA((len(smalls),)),
+            pltpu.VMEM((positions, hidden), low),
+            pltpu.VMEM((1, width), full),
+            pltpu.VMEM((1, width), full),
+            pltpu.SemaphoreType.DMA((5,)),
+            pltpu.SemaphoreType.DMA((5,)),
         ]
         + [scratch for sizes, _, _ in plan for scratch in ring_scratch(sizes, nodes, hidden)],
         compiler_params=pltpu.CompilerParams(
@@ -816,10 +936,9 @@
     nodes, lanes = ahead.nodes, ahead.lanes
 
     def each(method, *step):
-        getattr(ahead, method)(*step, 0)
+        for lane in range(lanes):
+            getattr(ahead, method)(*step, lane)
         getattr(behind, method)(*step)
-        for lane in range(1, lanes):
-            getattr(ahead, method)(*step, lane)
 
     for lane in range(1, lanes):
         ahead.towards(1, lane)

time: 201 us -> 197 us (0.980)
  Pallas kernels: 200 us -> 196 us
    pallas_call x1, Pallas kernels: 191 us -> 186 us  [run_blocks(): pl.pallas_call(functools.partial(blocks_kernel, edge, plan), out_shape=(j...]
where the time goes in v2:
time: 197 us; the launch traced here: 196 us
  Pallas kernels  196 us (99%)
    pallas_call x1, Pallas kernels, run_blocks(): pl.pallas_call(functools.partial(blocks_kernel, edge, plan), out_shape=(j...  186 us
    pallas_call x1, Pallas kernels, finish(): pl.pallas_call(functools.partial(finish_kernel, base), out_shape=out, in_...  9.18 us

profile of v2, /device:TPU:0, one launch (start us, length us, event | category | flops | bytes accessed | tf_op | source)
XLA Modules:
  0.0 196.5 jit_solution(14498013303691374672)
XLA Ops:
  0.7 186.5 %shard_map.280 = (bf16[1,4,256,1280]{3,2,1,0:T(8,128)(2,1)}, bf16[5888,640]{1,0:T(8,128)(2,1)}, f32[16,1280]{1,0:T(8,128)}) custom-call(bf16[1,4,256,1280]{3,2,1,0:T(8,128)(2,1)} %boundary.1, s32[4,4]{1,0:T(4,128)} %lengths.1, s32[4,256]{1,0:T(4,128)} %masked_in.1, s32[4,256]{1,0:T(4,128)} %residues_in.1, bf16[30,1280]{1,0:T(8,128)(2,1)} %bitcast.3, ...), custom_call_target="tpu_custom_call" | custom-call | tf_op jit(solution)/shard_map/pallas_call | solution.py:702
  187.1 9.2 %shard_map.281 = (bf16[1,4,256,1280]{3,2,1,0:T(8,128)(2,1)}, f32[1,1280,640]{2,1,0:T(8,128)}, f32[1,5,640,640]{3,2,1,0:T(8,128)}, f32[1,640,1280]{2,1,0:T(8,128)...) custom-call(bf16[1,4,256,1280]{3,2,1,0:T(8,128)(2,1)} %get-tuple-ele, ...), custom_call_target="tpu_custom_call" | custom-call | tf_op jit(solution)/shard_map/pallas_call | solution.py:1084

commit v3 on v2

--- a/solution.py
+++ b/solution.py
@@ -432,6 +432,10 @@
         for lane in range(1, rings[0].lanes):
             rings[0].towards(0, lane, True)
 
+    def later_lanes():
+        for lane in range(1, rings[0].lanes):
+            rings[0].towards(1, lane)
+
     def step(i, carry):
         fronts = i < rows
         m_start = jnp.where(leading, i - rows, i)
@@ -543,6 +547,7 @@
             back_last(m_end, whole[0])
             give(hat1, m_end).start()
             pl.when(i == 2 * rows)(other_lanes)
+            pl.when(i == 2 * rows + 1)(later_lanes)
 
         @pl.when(trailing & on(m_end))
         def _():
@@ -569,6 +574,7 @@
         def _():
             rings[0].towards(1, 0)
             rings[0].exchange(3)
+            later_lanes()
 
         @pl.when(final | (leading & (i == 2 * rows + 1)))
         def _():
@@ -940,8 +946,6 @@
             getattr(ahead, method)(*step, lane)
         getattr(behind, method)(*step)
 
-    for lane in range(1, lanes):
-        ahead.towards(1, lane)
     for step in (2, 3):
         ahead.exchange(step + 2)
         behind.exchange(2 * step - 2)

time: 197 us -> 196 us (level)
  no operation moved by 1% of the time
where the time goes in v3:
time: 196 us
  Pallas kernels  195 us (99%)
    pallas_call x1, Pallas kernels, run_blocks(): pl.pallas_call(functools.partial(blocks_kernel, edge, plan), out_shape=(j...  186 us
    pallas_call x1, Pallas kernels, finish(): pl.pallas_call(functools.partial(finish_kernel, base), out_shape=out, in_...  9.18 us

profile of v3, /device:TPU:0, one launch (start us, length us, event | category | flops | bytes accessed | tf_op | source)
XLA Modules:
  0.0 195.9 jit_solution(4356212599799182999)
XLA Ops:
  0.7 185.9 %shard_map.280 = (bf16[1,4,256,1280]{3,2,1,0:T(8,128)(2,1)}, bf16[5888,640]{1,0:T(8,128)(2,1)}, f32[16,1280]{1,0:T(8,128)}) custom-call(bf16[1,4,256,1280]{3,2,1,0:T(8,128)(2,1)} %boundary.1, s32[4,4]{1,0:T(4,128)} %lengths.1, s32[4,256]{1,0:T(4,128)} %masked_in.1, s32[4,256]{1,0:T(4,128)} %residues_in.1, bf16[30,1280]{1,0:T(8,128)(2,1)} %bitcast.3, ...), custom_call_target="tpu_custom_call" | custom-call | tf_op jit(solution)/shard_map/pallas_call | solution.py:708
  186.6 9.2 %shard_map.281 = (bf16[1,4,256,1280]{3,2,1,0:T(8,128)(2,1)}, f32[1,1280,640]{2,1,0:T(8,128)}, f32[1,5,640,640]{3,2,1,0:T(8,128)}, f32[1,640,1280]{2,1,0:T(8,128)...) custom-call(bf16[1,4,256,1280]{3,2,1,0:T(8,128)(2,1)} %get-tuple-ele, ...), custom_call_target="tpu_custom_call" | custom-call | tf_op jit(solution)/shard_map/pallas_call | solution.py:1088
